TPU v7x, 256 devices: a whole 4x4x8 slice. The times are simulated.
256 devices in a mesh: region: 8 (over y, x_hi), view: 32 (over z, x_lo, core).
Axes of the slice: x: 4 (x_hi: 2, x_lo: 2; x = x_hi * 2 + x_lo), y: 4, z: 8, core: 2. Of those that a mesh axis runs over, the one named last changes fastest.
Arguments:
- hidden: bfloat16 [32768, 1152], P(('region', 'view')), may hold values from -12 to 12, as said below
- pairs: int32 [1024, 2], replicated, may hold values from -1 to 255, as said below
- w_query: bfloat16 [1152, 1152], replicated, may hold values from -0.1875 to 0.1875
- w_key: bfloat16 [1152, 1152], replicated, may hold values from -0.1875 to 0.1875
- w_value: bfloat16 [1152, 1152], replicated, may hold values from -0.1875 to 0.1875
- w_out: bfloat16 [1152, 1152], replicated, may hold values from -0.1875 to 0.1875
Outputs:
- attended: bfloat16 [32768, 1152], P(('region', 'view'))
Inputs may be any that keep to these rules, and one draw needn't show every extreme that they name: hidden is of order one per entry. `pairs`: A row is either (-1, -1), which lists nothing, or (g, g2) with g < g2: either g2 = g + 32 in the next region with the same place in it, or g2 lies in g's region and its place minus g's place, taken modulo 32, is 1, 6 or 32 // 2 (or the same with g and g2 exchanged). Every view is linked with the view of its region whose place differs by 16. No pair is listed twice, and no view is linked to more than 8 others.
All inputs are finite; a program needn't handle non-finite values.
Results may differ from a plain program's by a relative error of at most 0.012.
The roundings to bfloat16 on the way count: a program that leaves them out, or rounds other values in their place, can miss the bound.
Values may be sent and summed in bfloat16 or wider, within the bound.
A program may use at most 192 MiB of HBM per device.

v0:
```python
import jax
import jax.numpy as jnp
from jax import lax
from jax.sharding import PartitionSpec as P

HEADS = 16
HEAD_SIZE = 72


neg_big = -1e30


def padded(x, sides, width):
    for axis, dim in sides:
        size, length = (lax.axis_size(axis), x.shape[dim])
        up = [(i, (i + 1) % size) for i in range(size - 1)]
        down = [(j, i) for i, j in up]
        last = lax.slice_in_dim(x, length - width, length, axis=dim)
        first = lax.slice_in_dim(x, 0, width, axis=dim)
        before = lax.ppermute(last, axis, up)
        after = lax.ppermute(first, axis, down)
        x = jnp.concatenate([before, x, after], axis=dim)
    return x


def attend(state, query, keys, values, allowed):
    maxima, totals, accum = state
    rows = keys.shape[0]
    heads = query.shape[0]
    key_heads = keys.reshape(rows, heads, -1)
    value_heads = values.reshape(rows, heads, -1)
    scores = jnp.einsum("hqe,khe->hqk", query, key_heads, preferred_element_type=jnp.float32)
    scores = scores * query.shape[2] ** (-0.5)
    scores = jnp.where(allowed[None, None, :], scores, neg_big)
    newtop = jnp.maximum(maxima, jnp.max(scores, axis=2))
    shrink = jnp.exp(maxima - newtop)
    weights = jnp.exp(scores - newtop[:, :, None])
    totals = totals * shrink + jnp.sum(weights, axis=2)
    summed = jnp.einsum(
        "hqk,khe->hqe",
        weights.astype(jnp.bfloat16),
        value_heads,
        preferred_element_type=jnp.float32,
    )
    accum = accum * shrink[:, :, None] + summed
    return (newtop, totals, accum)


def per_device(hidden, pairs, w_query, w_key, w_value, w_out):
    views = lax.axis_size("view")
    tokens = hidden.shape[0]
    region = lax.axis_index("region")
    place = lax.axis_index("view")
    myself = region * views + place

    def project(rows, weight):
        return jnp.dot(rows, weight, preferred_element_type=jnp.float32).astype(jnp.bfloat16)

    query = project(hidden, w_query).reshape(tokens, HEADS, HEAD_SIZE).transpose(1, 0, 2)
    keys = project(hidden, w_key)
    values = project(hidden, w_value)
    first_col = pairs[:, 0]
    second_col = pairs[:, 1]
    peers = region * views + jnp.arange(views, dtype=jnp.int32)
    forward = (first_col[:, None] == myself) & (second_col[:, None] == peers[None, :])
    backward = (second_col[:, None] == myself) & (first_col[:, None] == peers[None, :])
    linked = jnp.any(forward | backward, axis=0) | (peers == myself)
    upward = myself + views
    downward = myself - views
    above = jnp.any(
        (first_col == myself) & (second_col == upward)
        | (second_col == myself) & (first_col == upward)
    )
    below = jnp.any(
        (first_col == myself) & (second_col == downward)
        | (second_col == myself) & (first_col == downward)
    )
    state = (
        jnp.full((HEADS, tokens), neg_big, jnp.float32),
        jnp.zeros((HEADS, tokens), jnp.float32),
        jnp.zeros((HEADS, tokens, HEAD_SIZE), jnp.float32),
    )
    everything = jnp.ones((tokens,), bool)
    piece = (
        lax.all_gather(keys, "view", axis=0, tiled=True),
        lax.all_gather(values, "view", axis=0, tiled=True),
    )
    blocks = lambda parts: parts
    count = piece[0].shape[0] // tokens

    def one(index, carry):
        parts = tuple(
            (lax.dynamic_slice_in_dim(member, index * tokens, tokens, 0) for member in piece)
        )
        return lax.cond(
            linked[index],
            lambda c: attend(c, query, *blocks(parts), everything),
            lambda c: c,
            carry,
        )

    state = lax.fori_loop(0, count, one, state)
    add_state = state
    stacked = jnp.stack([keys, values])[None]
    rims = padded(stacked, (("region", 0),), 1)
    add_state = attend(add_state, query, rims[2, 0], rims[2, 1], jnp.full((tokens,), above))
    state = attend(add_state, query, rims[0, 0], rims[0, 1], jnp.full((tokens,), below))
    maxima, totals, accum = state
    mixed = (accum / totals[:, :, None]).transpose(1, 0, 2).reshape(tokens, -1).astype(jnp.bfloat16)
    return jnp.dot(mixed, w_out, preferred_element_type=jnp.float32).astype(jnp.bfloat16)


def solution(mesh):
    in_specs = (P(("region", "view"), None), P(), P(), P(), P(), P())
    out_specs = P(("region", "view"), None)
    return jax.shard_map(
        per_device, mesh=mesh, in_specs=in_specs, out_specs=out_specs, check_vma=False
    )
```

profile of v0, /device:TPU:16, one launch (start us, length us, event | category | flops | bytes accessed | tf_op | source)
XLA Modules:
  0.0 272.2 jit_solution(10327591106383799305)
XLA Ops:
  6.5 1.7 copy-done
  8.3 2.3 convolution_convert_fusion.3
  10.7 3.1 %convolution_convert_fusion.1 = bf16[128,1152]{1,0:T(8,128)(2,1)} fusion(bf16[128,1152]{1,0:T(8,128)(2,1)S(1)} %copy-done.3, bf16[1152,1152]{1,0:T(8,128)(2,1)} %param.14), kind=kOutput, calls=%fused_computation.12 | convolution fusion | flops 339886080 | bytes 3244032 | tf_op jit(solution)/shard_map/dot_general | solution.py:57
  13.8 1.8 maximum_bitcast_fusion
  15.6 4.9 %collective-permute-start.1 = (bf16[1,2,128,1152]{3,2,1,0:T(8,128)(2,1)}, bf16[1,2,128,1152]{3,2,1,0:T(8,128)(2,1)}, u32[]{:S(2)}, u32[]{:S(2)}) collective-permute-start(bf16[1,2,128,1152]{3,2,1,0:T(8,128)(2,1)} %maximum_bitcast_fusion), channel_id=1, source_target_pairs={{0,32},{32,64},{64,96},{96,128},{128,160},{160,192},{192,224},{1,3... | collective-permute-start | bytes 1769480 | tf_op jit(solution)/shard_map/ppermute | solution.py:20
  20.6 3.3 %collective-permute-start = (bf16[1,2,128,1152]{3,2,1,0:T(8,128)(2,1)}, bf16[1,2,128,1152]{3,2,1,0:T(8,128)(2,1)}, u32[]{:S(2)}, u32[]{:S(2)}) collective-permute-start(bf16[1,2,128,1152]{3,2,1,0:T(8,128)(2,1)} %maximum_bitcast_fusion), channel_id=1, source_target_pairs={{32,0},{64,32},{96,64},{128,96},{160,128},{192,160},{224,192},{33,... | collective-permute-start | bytes 1769480 | tf_op jit(solution)/shard_map/ppermute | solution.py:21
  23.9 2.4 convolution_convert_fusion.2
  28.1 15.8 %collective-permute-done.1 = bf16[1,2,128,1152]{3,2,1,0:T(8,128)(2,1)} collective-permute-done((bf16[1,2,128,1152]{3,2,1,0:T(8,128)(2,1)}, bf16[1,2,128,1152]{3,2,1,0:T(8,128)(2,1)}, u32[]{:S(2)}, u32[]{:S(2)}) %collective-permute-start.1) | collective-permute-done | bytes 589856 | tf_op jit(solution)/shard_map/ppermute | solution.py:20
  46.1 21.7 %collective-permute-done = bf16[1,2,128,1152]{3,2,1,0:T(8,128)(2,1)} collective-permute-done((bf16[1,2,128,1152]{3,2,1,0:T(8,128)(2,1)}, bf16[1,2,128,1152]{3,2,1,0:T(8,128)(2,1)}, u32[]{:S(2)}, u32[]{:S(2)}) %collective-permute-start) | collective-permute-done | bytes 589856 | tf_op jit(solution)/shard_map/ppermute | solution.py:21
  67.8 2.0 fusion.21
  69.8 1.2 copy.31
  71.0 1.8 copy.32
  72.8 2.6 fusion.24
  75.4 2.6 fusion.23
  78.1 25.3 %all-gather.3.cloned.1.call-done = bf16[4096,1152]{1,0:T(8,128)(2,1)} async-done(((bf16[128,1152]{1,0:T(8,128)(2,1)}), bf16[4096,1152]{1,0:T(8,128)(2,1)}) %all-gather.3.cloned.1.call-update) | async-done | bytes 9437200 | tf_op jit(solution)/shard_map/all_gather | solution.py:85
  103.3 12.7 %copy.29 = bf16[4096,1152]{0,1:T(8,128)(2,1)} copy(bf16[4096,1152]{1,0:T(8,128)(2,1)} %all-gather.3.cloned.1.call-done) | data formatting | bytes 18874368 | tf_op jit(solution)/shard_map/while | solution.py:102
  116.0 61.9 %all-gather.5.cloned.1.call-done = bf16[4096,1152]{1,0:T(8,128)(2,1)} async-done(((bf16[128,1152]{1,0:T(8,128)(2,1)}), bf16[4096,1152]{1,0:T(8,128)(2,1)}) %all-gather.5.cloned.1.call-update) | async-done | bytes 9437200 | tf_op jit(solution)/shard_map/all_gather | solution.py:86
  177.9 12.1 %copy.30 = bf16[4096,1152]{0,1:T(8,128)(2,1)} copy(bf16[4096,1152]{1,0:T(8,128)(2,1)} %all-gather.5.cloned.1.call-done) | data formatting | bytes 18874368 | tf_op jit(solution)/shard_map/while | solution.py:102
  190.0 69.4 %while.17 = (s32[]{:T(128)}, f32[16,128]{1,0:T(8,128)S(1)}, f32[16,128]{1,0:T(8,128)S(1)}, f32[16,128,72]{1,2,0:T(8,128)S(1)}, pred[32]{0:T(512)(128)(4,1)}, /*i...) while((s32[]{:T(128)}, f32[16,128]{1,0:T(8,128)S(1)}, ...), condition=%wide.region_6.7_spmd, body=%wide.region_1.6_spmd.sunk | while | flops 77369344 | bytes 6521106 | solution.py:102
  190.0 1.2 dynamic_slice.38
  191.8 2.2 conditional.2
  191.8 1.1 constant_dynamic-slice_fusion
  194.0 1.2 dynamic_slice.38
  195.8 2.2 conditional.2
  195.8 1.1 constant_dynamic-slice_fusion
  198.1 1.2 dynamic_slice.38
  199.9 1.2 dynamic_slice.38
  201.7 1.2 dynamic_slice.38
  203.5 1.2 dynamic_slice.38
  205.4 1.2 dynamic_slice.38
  207.2 2.2 conditional.2
  207.2 1.1 constant_dynamic-slice_fusion
  209.4 1.2 dynamic_slice.38
  211.2 1.2 dynamic_slice.38
  213.0 1.2 dynamic_slice.38
  214.9 1.2 dynamic_slice.38
  216.7 1.2 dynamic_slice.38
  218.5 1.2 dynamic_slice.38
  220.3 1.2 dynamic_slice.38
  222.2 1.2 dynamic_slice.38
  224.0 1.2 dynamic_slice.38
  225.8 1.2 dynamic_slice.38
  227.6 2.2 conditional.2
  227.6 1.1 constant_dynamic-slice_fusion
  229.8 1.2 dynamic_slice.38
  231.7 1.2 dynamic_slice.38
  233.5 1.2 dynamic_slice.38
  235.3 1.2 dynamic_slice.38
  237.1 1.2 dynamic_slice.38
  239.0 1.2 dynamic_slice.38
  240.8 1.2 dynamic_slice.38
  242.6 1.2 dynamic_slice.38
  244.4 1.2 dynamic_slice.38
  246.3 1.2 dynamic_slice.38
  248.1 1.2 dynamic_slice.38
  249.9 1.2 dynamic_slice.38
  251.7 1.2 dynamic_slice.38
  253.6 1.2 dynamic_slice.38
  255.4 1.2 dynamic_slice.38
  257.2 2.2 conditional.2
  257.2 1.1 constant_dynamic-slice_fusion
  260.3 1.9 fusion.10
  262.2 1.4 fusion.8
  264.1 1.3 convolution_convert_fusion
  (92 shorter events, 11.0 us)
Async XLA Ops:
  6.5 1.8 copy-start
  6.5 4.1 %copy-start.3 = (bf16[128,1152]{1,0:T(8,128)(2,1)S(1)}, bf16[128,1152]{1,0:T(8,128)(2,1)}, u32[]{:S(2)}) copy-start(bf16[128,1152]{1,0:T(8,128)(2,1)} %param.10) | copy-start | bytes 884740
  6.5 96.8 %all-gather.3.cloned.1.call-start = ((), (), s32[]{:S(2)}) async-start(), calls=%async_computation | async-start | bytes 9732096 | tf_op jit(solution)/shard_map/all_gather | solution.py:85
  10.6 3.2 %copy-start.4 = (bf16[128,1152]{1,0:T(8,128)(2,1)S(1)}, bf16[128,1152]{1,0:T(8,128)(2,1)}, u32[]{:S(2)}) copy-start(bf16[128,1152]{1,0:T(8,128)(2,1)} %convolution_convert_fusion.3) | copy-start | bytes 884740
  10.6 13.3 %copy-start.7 = (s32[1024,2]{0,1:T(2,128)S(1)}, s32[1024,2]{0,1:T(2,128)}, u32[]{:S(2)}) copy-start(s32[1024,2]{0,1:T(2,128)} %param.11) | copy-start | bytes 24580
  10.6 167.2 %all-gather.5.cloned.1.call-start = ((), (), s32[]{:S(2)}) async-start(), calls=%async_computation.1 | async-start | bytes 9732096 | tf_op jit(solution)/shard_map/all_gather | solution.py:86
  15.6 28.3 %collective-permute-start.1 = (bf16[1,2,128,1152]{3,2,1,0:T(8,128)(2,1)}, bf16[1,2,128,1152]{3,2,1,0:T(8,128)(2,1)}, u32[]{:S(2)}, u32[]{:S(2)}) collective-permute-start(bf16[1,2,128,1152]{3,2,1,0:T(8,128)(2,1)} %maximum_bitcast_fusion), channel_id=1, source_target_pairs={{0,32},{32,64},{64,96},{96,128},{128,160},{160,192},{192,224},{1,3... | collective-permute-start | bytes 1769480 | tf_op jit(solution)/shard_map/ppermute | solution.py:20
  20.6 47.3 %collective-permute-start = (bf16[1,2,128,1152]{3,2,1,0:T(8,128)(2,1)}, bf16[1,2,128,1152]{3,2,1,0:T(8,128)(2,1)}, u32[]{:S(2)}, u32[]{:S(2)}) collective-permute-start(bf16[1,2,128,1152]{3,2,1,0:T(8,128)(2,1)} %maximum_bitcast_fusion), channel_id=1, source_target_pairs={{32,0},{64,32},{96,64},{128,96},{160,128},{192,160},{224,192},{33,... | collective-permute-start | bytes 1769480 | tf_op jit(solution)/shard_map/ppermute | solution.py:21
  259.4 2.8 %copy-start.1 = (f32[16,128,128]{1,2,0:T(8,128)S(1)}, f32[16,128,128]{1,2,0:T(8,128)}, u32[]{:S(2)}) copy-start(f32[16,128,128]{1,2,0:T(8,128)} %get-tuple-element.327) | copy-start | bytes 3145732
  259.4 4.3 %copy-start.2 = (f32[16,128,128]{1,2,0:T(8,128)S(1)}, f32[16,128,128]{1,2,0:T(8,128)}, u32[]{:S(2)}) copy-start(f32[16,128,128]{1,2,0:T(8,128)} %get-tuple-element.325) | copy-start | bytes 3145732
  259.4 4.3 %copy-start.6 = (bf16[1,1,128,1152]{2,3,1,0:T(8,128)(2,1)S(1)}, bf16[1,1,128,1152]{2,3,1,0:T(8,128)(2,1)}, u32[]{:S(2)}) copy-start(bf16[1,1,128,1152]{2,3,1,0:T(8,128)(2,1)} %copy.35) | copy-start | bytes 884740
  262.2 1.8 copy-start.5
Sparse Core Ops, SparseCore 0:
  10.7 92.5 all-gather.2
  105.2 72.6 all-gather.4
where the time goes:
time: 278 us; the launch traced here: 272 us
  waiting for transfers between devices  125 us (45%)
  local copies, waits for them, and re-layouts  78.6 us (28%)
  matrix products  20.4 us (7%)
  loops' own time  19.6 us (7%)
  between operations  13.6 us (5%)
  starting transfers between devices  8.28 us (3%)
  other arithmetic  7.04 us (3%)
    all_gather x1, waiting for transfers between devices, per_device(): lax.all_gather(values, 'view', axis=0, tiled=True)  61.9 us
    dynamic_slice x32, local copies, waits for them, and re-layouts, one(): linked[index]  39 us
    all_gather x1, waiting for transfers between devices, per_device(): lax.all_gather(keys, 'view', axis=0, tiled=True)  25.3 us
    while x2, local copies, waits for them, and re-layouts, per_device(): state = lax.fori_loop(0, count, one, state)  24.8 us
    ppermute x1, waiting for transfers between devices, padded(): after = lax.ppermute(first, axis, down)  21.7 us
    another operation x1, loops' own time, per_device(): state = lax.fori_loop(0, count, one, state)  18.9 us
    ppermute x1, waiting for transfers between devices, padded(): before = lax.ppermute(last, axis, up)  15.8 us
    dot_general x3, matrix products, project(): jnp.dot(rows, weight, preferred_element_type=jnp.float32)  7.75 us
  transfers between devices with their start and end apart: 4, of which 4 were waited for; matrix products, arithmetic and copies ran while one was open for 13% of the time, Pallas kernels for 0%

commit v1 on v0

v1 whole, which is shorter than its diff:
```python
import functools

import jax
import jax.numpy as jnp
import numpy as np
from jax import lax
from jax.experimental import pallas as pl
from jax.experimental.pallas import tpu as pltpu
from jax.sharding import PartitionSpec as P

MESH = pl.DeviceIdType.MESH
BF, F32 = jnp.bfloat16, jnp.float32
D, TOK, HEADS, HEAD = 1152, 128, 16, 72
NEG = -1e30
SCALE2 = float(HEAD**-0.5 * np.log2(np.e))
NT = (((1,), (1,)), ((), ()))

WINDOWS = ((0, (0, 1, 2)), (1, (3, 4)), (2, (5, 6)), (3, (7,)), (4, (8, 9)), (5, (10, 11)), (6, (12, 13)), (7, (14, 15)))

OWN, SIB, STEP1, REG1, REG2, NEAR6, FAR6, HALF = range(8)

CHUNKS = ((0, 640, "a"), (640, 512, "b"))
GROUPS = ((OWN, SIB), (STEP1, REG1), (REG2, NEAR6), (FAR6,), (HALF,))


class Moves:
    def __init__(self, hidden, held, over, half_a, sends, recvs):
        r, p = lax.axis_index("region"), lax.axis_index("view")
        y, xh = r // 2, lax.rem(r, 2)
        z, col, core = p // 4, lax.rem(p // 2, 2), lax.rem(p, 2)
        f = 2 * col - 1
        self.sends, self.recvs, self.table = sends, recvs, {}

        def at(dz, column, c):
            return (r, lax.rem(z + dz + 8, 8) * 4 + column * 2 + c)

        other = 1 - col
        dy = 1 - 2 * xh
        self.cross = core != col
        self.has_to = (y + dy >= 0) & (y + dy <= 3)
        self.has_from = (y - dy >= 0) & (y - dy <= 3)
        sib, flip = at(0, col, 1 - core), at(0, other, core)
        xpair = (y * 2 + 1 - xh, z * 4 + other * 2 + core)
        y_to = (jnp.clip(y + dy, 0, 3) * 2 + xh, p)
        y_from = (jnp.clip(y - dy, 0, 3) * 2 + xh, p)
        step_to, step_from = at(-f, col, 1 - core), at(f, col, 1 - core)

        self.greet = [sib, flip, xpair, at(-f, col, core), at(2 * f, col, core), at(-2 * f, col, core), at(-2 * f, other, core)]
        self.greet_if = [(jnp.logical_not(self.cross), step_from), (self.has_from, y_from)]
        self.partners = 7 + self.cross.astype(jnp.int32) + self.has_to.astype(jnp.int32)

        place = lambda region, dev: region * 32 + dev[1]
        self.me = r * 32 + p
        nowhere = jnp.int32(-7)
        self.views = {
            SIB: place(r, sib),
            STEP1: jnp.where(self.cross, place(r, at(0, other, 1 - core)), place(r, at(f, other, 1 - core))),
            REG1: (y * 2 + 1 - xh) * 32 + p,
            REG2: jnp.where(self.has_from, ((y - dy) * 2 + 1 - xh) * 32 + p, nowhere),
            NEAR6: place(r, at(-f, other, core)),
            FAR6: place(r, at(2 * f, other, core)),
            HALF: place(r, at(4, col, core)),
        }

        slot = lambda i: held.at[pl.ds(i * TOK, TOK)]
        self.add("sib", hidden, slot(SIB), sib)
        for k, (first, size, kind) in enumerate(CHUNKS):
            cut = lambda ref: ref.at[:, pl.ds(first, size)]
            self.add(("flip", k), cut(hidden), cut(over), flip)
            if kind == "a":
                self.add(("two", k), cut(hidden), half_a, at(2 * f, col, core))
                self.add(("four", k), half_a, cut(slot(HALF)), at(2 * f, col, core))
                self.add(("side", k), half_a, cut(slot(FAR6)), flip)
            else:
                self.add(("two", k), cut(over), cut(slot(FAR6)), at(-2 * f, col, core))
                self.add(("four", k), cut(slot(FAR6)), cut(slot(HALF)), at(-2 * f, other, core))
            self.add(("near", k), cut(over), cut(slot(NEAR6)), at(f, col, core))
            self.add(("step", k), cut(over), cut(slot(STEP1)), sib, step_to)
            self.add(("xpair", k), cut(over), cut(slot(REG1)), xpair)
            self.add(("ypair", k), cut(slot(REG1)), cut(slot(REG2)), y_to)

    def add(self, key, src, dst, device, device_if_cross=None):
        i = len(self.table)
        make = lambda to: pltpu.make_async_remote_copy(
            src_ref=src, dst_ref=dst, send_sem=self.sends.at[i], recv_sem=self.recvs.at[i], device_id=to, device_id_type=MESH
        )
        self.table[key] = (make, device, device_if_cross)

    def start(self, key):
        make, device, device_if_cross = self.table[key]
        if device_if_cross is not None:
            @pl.when(self.cross)
            def _():
                make(device_if_cross).start()

            @pl.when(jnp.logical_not(self.cross))
            def _():
                make(device).start()
        elif key[0] == "ypair":
            @pl.when(self.has_to)
            def _():
                make(device).start()
        else:
            make(device).start()

    def arrived(self, key):
        make, device, _ = self.table[key]
        if key[0] == "ypair":
            @pl.when(self.has_from)
            def _():
                make(device).wait_recv()
        else:
            make(device).wait_recv()

    def sent(self, key):
        make, device, _ = self.table[key]
        if key[0] == "ypair":
            @pl.when(self.has_to)
            def _():
                make(device).wait_send()
        else:
            make(device).wait_send()

    def barrier(self):
        sem = pltpu.get_barrier_semaphore()
        tell = lambda dev: pl.semaphore_signal(sem, inc=1, device_id=dev, device_id_type=MESH)
        for dev in self.greet:
            tell(dev)
        for cond, dev in self.greet_if:
            @pl.when(cond)
            def _(dev=dev):
                tell(dev)
        return lambda: pl.semaphore_wait(sem, self.partners)


def project(rows, weight):
    return jnp.dot(rows, weight, preferred_element_type=F32)


def make_queries(x, wq, queries):
    q = project(x, wq[...])
    row = 0
    for tile, heads in WINDOWS:
        part = q[:, tile * 128 : tile * 128 + 256]
        lane = lax.broadcasted_iota(jnp.int32, (TOK, 256), 1) + tile * 128
        for h in heads:
            keep = (lane >= h * HEAD) & (lane < (h + 1) * HEAD)
            queries[row : row + TOK, :] = jnp.where(keep, part, 0.0).astype(BF)
            row += TOK


def attend(first, at, links, queries, keys, values_t, tops, totals, accum, scores, weights):
    m = len(links) * TOK
    row = 0
    for tile, heads in WINDOWS:
        n = len(heads) * TOK
        scores[:m, row : row + n] = lax.dot_general(
            keys[at : at + m, tile * 128 : tile * 128 + 256], queries[row : row + n, :], NT, preferred_element_type=F32
        )
        row += n
    shrink, newtops = [], []
    for h in range(HEADS):
        top = None
        for b, link in enumerate(links):
            x = jnp.max(scores[b * TOK : (b + 1) * TOK, h * TOK : (h + 1) * TOK], axis=0, keepdims=True)
            if link is not None:
                x = jnp.where(link, x, NEG)
            top = x if top is None else jnp.maximum(top, x)
        if not first:
            old = tops[h : h + 1, :]
            top = jnp.maximum(old, top)
            shrink.append(jnp.exp2((old - top) * SCALE2))
        newtops.append(top)
    for h in range(HEADS):
        total = None
        for b, link in enumerate(links):
            x = scores[b * TOK : (b + 1) * TOK, h * TOK : (h + 1) * TOK]
            top = newtops[h] if link is None else jnp.where(link, newtops[h], -NEG)
            w = jnp.exp2((x - top) * SCALE2)
            weights[b * TOK : (b + 1) * TOK, h * TOK : (h + 1) * TOK] = w.astype(BF)
            w = jnp.sum(w, axis=0, keepdims=True)
            total = w if total is None else total + w
        tops[h : h + 1, :] = newtops[h]
        totals[h : h + 1, :] = total if first else totals[h : h + 1, :] * shrink[h] + total
    for h in range(HEADS):
        start = HEAD * h - (8 if h % 2 else 0)
        o = jnp.dot(values_t[start : start + 80, at : at + m], weights[:m, h * TOK : (h + 1) * TOK], preferred_element_type=F32)
        o = o[8:80] if h % 2 else o[:72]
        accum[h] = o if first else accum[h] * shrink[h] + o


def finish(totals, accum, mixed_t, wo):
    for h in range(HEADS):
        mixed_t[h * HEAD : (h + 1) * HEAD, :] = accum[h] / totals[h : h + 1, :]
    mixed = jnp.concatenate([mixed_t[t * 128 : (t + 1) * 128, :].T.astype(BF) for t in range(D // 128)], axis=1)
    return project(mixed, wo[...]).astype(BF)


PROGRAM = (
    ("send", ("two", 0), ("flip", 1), ("flip", 0), "sib"),
    "links", "q", ("kv", (OWN,)),
    ("relay", ("flip", 1), ("two", 1), ("near", 1), ("step", 1), ("xpair", 1)),
    ("get", "sib"), ("kv", (SIB,)),
    ("relay", ("two", 0), ("four", 0), ("side", 0)),
    ("relay", ("flip", 0), ("near", 0), ("step", 0), ("xpair", 0)),
    ("attend", 0),
    ("relay", ("two", 1), ("four", 1)),
    ("relay", ("xpair", 1), ("ypair", 1)),
    ("relay", ("xpair", 0), ("ypair", 0)),
    ("get", ("step", 0), ("step", 1)), ("kv", (STEP1, REG1)), ("attend", 1),
    ("get", ("ypair", 0), ("ypair", 1), ("near", 0), ("near", 1)), ("kv", (REG2, NEAR6)), ("attend", 2),
    ("get", ("side", 0)), ("kv", (FAR6,)), ("attend", 3),
    ("get", ("four", 0), ("four", 1)), ("kv", (HALF,)), ("attend", 4),
    "finish",
)


def kernel(
    hidden, pairs, w_query, w_key, w_value, w_out, out,
    held, over, half_a, wq, wk, wv, wo, wvt, queries, keys, values_t, tops, totals, accum, scores, weights, mixed_t,
    sends, recvs, local,
):
    moves = Moves(hidden, held, over, half_a, sends, recvs)
    wait_barrier = moves.barrier()
    loads = {
        name: pltpu.make_async_copy(src, dst, local.at[i])
        for i, (name, src, dst) in enumerate(
            (("x", hidden, held.at[pl.ds(0, TOK)]), ("wq", w_query, wq), ("wk", w_key, wk), ("wv", w_value, wv), ("wo", w_out, wo))
        )
    }
    for load in loads.values():
        load.start()

    @pl.when(jnp.logical_not(moves.has_from))
    def _():
        held[REG2 * TOK : (REG2 + 1) * TOK, :] = jnp.zeros((TOK, D), BF)

    wait_barrier()
    links = {OWN: None}
    for step in PROGRAM:
        verb, args = (step, ()) if isinstance(step, str) else (step[0], step[1:])
        if verb == "send":
            for key in args:
                moves.start(key)
        elif verb == "relay":
            moves.arrived(args[0])
            for key in args[1:]:
                moves.start(key)
        elif verb == "get":
            for key in args:
                moves.arrived(key)
        elif verb == "links":
            low, high = pairs[0:1, :], pairs[1:2, :]
            for slot, view in moves.views.items():
                hit = ((low == moves.me) & (high == view)) | ((low == view) & (high == moves.me))
                any_hit = jnp.max(jnp.where(hit, 1.0, 0.0), axis=1, keepdims=True)
                links[slot] = jnp.broadcast_to(any_hit, (1, TOK)) > 0.5
        elif verb == "q":
            loads["x"].wait()
            loads["wq"].wait()
            make_queries(held[:TOK, :], wq, queries)
        elif verb == "kv":
            slots = args[0]
            if slots == (OWN,):
                loads["wk"].wait()
            rows = slice(slots[0] * TOK, (slots[-1] + 1) * TOK)
            keys[rows, :] = project(held[rows, :], wk[...]).astype(BF)
            if slots == (OWN,):
                loads["wv"].wait()
                for i in range(D // 128):
                    wvt[i * 128 : (i + 1) * 128, :] = wv[:, i * 128 : (i + 1) * 128].T
            values_t[:, rows] = lax.dot_general(wvt[...], held[rows, :], NT, preferred_element_type=F32).astype(BF)
        elif verb == "attend":
            slots = GROUPS[args[0]]
            attend(
                args[0] == 0, slots[0] * TOK, [links[s] for s in slots],
                queries, keys, values_t, tops, totals, accum, scores, weights,
            )
        elif verb == "finish":
            loads["wo"].wait()
            out[...] = finish(totals, accum, mixed_t, wo)
    for key in moves.table:
        moves.sent(key)


def per_device(hidden, pairs, w_query, w_key, w_value, w_out):
    any_space, vmem = pl.BlockSpec(memory_space=pl.ANY), pl.BlockSpec(memory_space=pltpu.VMEM)
    half = sum(size for _, size, kind in CHUNKS if kind == "a")
    bf = lambda *shape: pltpu.VMEM(shape, BF)
    f32 = lambda *shape: pltpu.VMEM(shape, F32)
    return pl.pallas_call(
        kernel,
        out_shape=jax.ShapeDtypeStruct((TOK, D), BF),
        in_specs=[any_space, vmem, any_space, any_space, any_space, any_space],
        out_specs=vmem,
        scratch_shapes=[
            bf(8 * TOK, D), bf(TOK, D), bf(TOK, half),
            bf(D, D), bf(D, D), bf(D, D), bf(D, D), bf(D, D),
            bf(HEADS * TOK, 256), bf(8 * TOK, D), bf(D, 8 * TOK),
            f32(HEADS, TOK), f32(HEADS, TOK), f32(HEADS, HEAD, TOK),
            f32(2 * TOK, HEADS * TOK), bf(2 * TOK, HEADS * TOK), f32(D, TOK),
            pltpu.SemaphoreType.DMA((32,)), pltpu.SemaphoreType.DMA((32,)), pltpu.SemaphoreType.DMA((5,)),
        ],
        compiler_params=pltpu.CompilerParams(collective_id=0, has_side_effects=True, vmem_limit_bytes=60 * 2**20),
        name="cross_view_attention",
    )(hidden, pairs.T, w_query, w_key, w_value, w_out)


def solution(mesh):
    in_specs = (P(("region", "view"), None), P(), P(), P(), P(), P())
    return jax.shard_map(
        per_device, mesh=mesh, in_specs=in_specs, out_specs=P(("region", "view"), None), check_vma=False
    )
```

time: 278 us -> 40.6 us (0.15); the launches traced: 272 us -> 40.3 us
  waiting for transfers between devices: 125 us -> 0 us
  local copies, waits for them, and re-layouts: 78.6 us -> 1.7 us
  Pallas kernels: 0 us -> 38.5 us
  matrix products: 20.4 us -> 0 us
  loops' own time: 19.6 us -> 0 us
  between operations: 13.6 us -> 0.01 us
  starting transfers between devices: 8.28 us -> 0 us
  other arithmetic: 7.04 us -> 0 us
    all_gather x2 -> x0, waiting for transfers between devices: 87.1 us -> none  [the longest x1 61.9 us: per_device(): lax.all_gather(values, 'view', axis=0, tiled=True)]
    dynamic_slice x37 -> x0, local copies, waits for them, and re-layouts: 44.5 us -> none  [the longest x32 39 us: one(): linked[index]]
    pallas_call x0 -> x1, Pallas kernels: none -> 38.5 us  [per_device(): pl.pallas_call(kernel, out_shape=jax.ShapeDtypeStruct((TOK, D), BF), in_s...]
    ppermute x2 -> x0, waiting for transfers between devices: 37.6 us -> none  [the longest x1 21.7 us: padded(): after = lax.ppermute(first, axis, down)]
    while x2 -> x0, local copies, waits for them, and re-layouts: 24.8 us -> none  [per_device(): state = lax.fori_loop(0, count, one, state)]
    dot_general x18 -> x0, matrix products: 20.4 us -> none  [the longest x3 7.75 us: project(): jnp.dot(rows, weight, preferred_element_type=jnp.float32)]
    another operation x33 -> x0, loops' own time: 19.6 us -> none  [the longest x1 18.9 us: per_device(): state = lax.fori_loop(0, count, one, state)]
    ppermute x2 -> x0, starting transfers between devices: 8.24 us -> none  [the longest x1 4.93 us: padded(): before = lax.ppermute(last, axis, up)]
  transfers between devices with their start and end apart: 4 -> 0, of which waited for: 4 -> 0; matrix products, arithmetic and copies ran while one was open for 13% -> 0% of each run, Pallas kernels for 0% -> 0%
where the time goes in v1:
time: 40.6 us; the launch traced here: 40.3 us
  Pallas kernels  38.5 us (95%)
  local copies, waits for them, and re-layouts  1.7 us (4%)
    pallas_call x1, Pallas kernels, per_device(): pl.pallas_call(kernel, out_shape=jax.ShapeDtypeStruct((TOK, D), BF), in_s...  38.5 us
    unnamed x1, local copies, waits for them, and re-layouts  1.7 us

profile of v1, /device:TPU:16, one launch (start us, length us, event | category | flops | bytes accessed | tf_op | source)
XLA Modules:
  0.0 40.3 jit_solution(5388013462442880472)
XLA Ops:
  0.0 38.5 %cross_view_attention.1 = bf16[128,1152]{1,0:T(8,128)(2,1)} custom-call(bf16[128,1152]{1,0:T(8,128)(2,1)} %hidden.1, s32[2,1024]{1,0:T(2,128)} %bitcast.1, bf16[1152,1152]{1,0:T(8,128)(2,1)} %w_query.1, bf16[1152,1152]{1,0:T(8,128)(2,1)} %w_key.1, bf16[1152,1152]{1,0:T(8,128)(2,1)} %w_value.1, bf16[1152,1152]{1,0:T(8,128)(2,1)} %w_out.1), custom_call_target="tpu_custom_call" | custom-call | tf_op jit(solution)/shard_map/cross_view_attention/pallas_call | solution.py:291
  38.6 1.7 %copy.8 = bf16[128,1152]{1,0:T(8,128)(2,1)} copy(bf16[128,1152]{1,0:T(8,128)(2,1)} %cross_view_attention.1) | data formatting | bytes 589824

commit v2 on v1

--- a/solution.py
+++ b/solution.py
@@ -17,14 +17,14 @@
 
 WINDOWS = ((0, (0, 1, 2)), (1, (3, 4)), (2, (5, 6)), (3, (7,)), (4, (8, 9)), (5, (10, 11)), (6, (12, 13)), (7, (14, 15)))
 
-OWN, SIB, STEP1, REG1, REG2, NEAR6, FAR6, HALF = range(8)
-
-CHUNKS = ((0, 640, "a"), (640, 512, "b"))
-GROUPS = ((OWN, SIB), (STEP1, REG1), (REG2, NEAR6), (FAR6,), (HALF,))
+OWN, SIB, REG1, FAR6, STEP1, NEAR6, REG2, HALF = range(8)
+
+CHUNKS = ((0, 640, "a", "z"), (640, 512, "b", "x"))
+GROUPS = ((OWN, SIB), (REG1, FAR6), (STEP1, NEAR6), (REG2,), (HALF,))
 
 
 class Moves:
-    def __init__(self, hidden, held, over, half_a, sends, recvs):
+    def __init__(self, hidden, held, over, half_a, back, sends, recvs):
         r, p = lax.axis_index("region"), lax.axis_index("view")
         y, xh = r // 2, lax.rem(r, 2)
         z, col, core = p // 4, lax.rem(p // 2, 2), lax.rem(p, 2)
@@ -45,9 +45,9 @@
         y_from = (jnp.clip(y - dy, 0, 3) * 2 + xh, p)
         step_to, step_from = at(-f, col, 1 - core), at(f, col, 1 - core)
 
-        self.greet = [sib, flip, xpair, at(-f, col, core), at(2 * f, col, core), at(-2 * f, col, core), at(-2 * f, other, core)]
+        self.greet = [sib, flip, xpair, at(-f, col, core), at(f, col, core), at(2 * f, col, core), at(-2 * f, col, core), at(-2 * f, other, core)]
         self.greet_if = [(jnp.logical_not(self.cross), step_from), (self.has_from, y_from)]
-        self.partners = 7 + self.cross.astype(jnp.int32) + self.has_to.astype(jnp.int32)
+        self.partners = 8 + self.cross.astype(jnp.int32) + self.has_to.astype(jnp.int32)
 
         place = lambda region, dev: region * 32 + dev[1]
         self.me = r * 32 + p
@@ -64,7 +64,7 @@
 
         slot = lambda i: held.at[pl.ds(i * TOK, TOK)]
         self.add("sib", hidden, slot(SIB), sib)
-        for k, (first, size, kind) in enumerate(CHUNKS):
+        for k, (first, size, kind, way) in enumerate(CHUNKS):
             cut = lambda ref: ref.at[:, pl.ds(first, size)]
             self.add(("flip", k), cut(hidden), cut(over), flip)
             if kind == "a":
@@ -74,7 +74,11 @@
             else:
                 self.add(("two", k), cut(over), cut(slot(FAR6)), at(-2 * f, col, core))
                 self.add(("four", k), cut(slot(FAR6)), cut(slot(HALF)), at(-2 * f, other, core))
-            self.add(("near", k), cut(over), cut(slot(NEAR6)), at(f, col, core))
+            if way == "z":
+                self.add(("back", k), cut(hidden), cut(back), at(-f, col, core))
+                self.add(("near", k), cut(back), cut(slot(NEAR6)), flip)
+            else:
+                self.add(("near", k), cut(over), cut(slot(NEAR6)), at(f, col, core))
             self.add(("step", k), cut(over), cut(slot(STEP1)), sib, step_to)
             self.add(("xpair", k), cut(over), cut(slot(REG1)), xpair)
             self.add(("ypair", k), cut(slot(REG1)), cut(slot(REG2)), y_to)
@@ -197,19 +201,21 @@
 
 
 PROGRAM = (
-    ("send", ("two", 0), ("flip", 1), ("flip", 0), "sib"),
-    "links", "q", ("kv", (OWN,)),
+    ("send", ("two", 0), ("flip", 1), ("flip", 0), ("back", 0), "sib"),
+    "links", "q",
+    ("key", (OWN,)), "turn",
     ("relay", ("flip", 1), ("two", 1), ("near", 1), ("step", 1), ("xpair", 1)),
-    ("get", "sib"), ("kv", (SIB,)),
+    ("relay", ("back", 0), ("near", 0)),
+    ("value", (OWN,)),
+    ("get", "sib"), ("kv", (SIB,)), ("attend", 0),
     ("relay", ("two", 0), ("four", 0), ("side", 0)),
-    ("relay", ("flip", 0), ("near", 0), ("step", 0), ("xpair", 0)),
-    ("attend", 0),
+    ("relay", ("flip", 0), ("step", 0), ("xpair", 0)),
+    ("relay", ("xpair", 1), ("ypair", 1)),
     ("relay", ("two", 1), ("four", 1)),
-    ("relay", ("xpair", 1), ("ypair", 1)),
     ("relay", ("xpair", 0), ("ypair", 0)),
-    ("get", ("step", 0), ("step", 1)), ("kv", (STEP1, REG1)), ("attend", 1),
-    ("get", ("ypair", 0), ("ypair", 1), ("near", 0), ("near", 1)), ("kv", (REG2, NEAR6)), ("attend", 2),
-    ("get", ("side", 0)), ("kv", (FAR6,)), ("attend", 3),
+    ("get", ("side", 0)), ("kv", (REG1, FAR6)), ("attend", 1),
+    ("get", ("step", 0), ("step", 1), ("near", 0), ("near", 1)), ("kv", (STEP1, NEAR6)), ("attend", 2),
+    ("get", ("ypair", 0), ("ypair", 1)), ("kv", (REG2,)), ("attend", 3),
     ("get", ("four", 0), ("four", 1)), ("kv", (HALF,)), ("attend", 4),
     "finish",
 )
@@ -217,10 +223,10 @@
 
 def kernel(
     hidden, pairs, w_query, w_key, w_value, w_out, out,
-    held, over, half_a, wq, wk, wv, wo, wvt, queries, keys, values_t, tops, totals, accum, scores, weights, mixed_t,
+    held, over, half_a, back, wq, wk, wv, wo, wvt, queries, keys, values_t, tops, totals, accum, scores, weights, mixed_t,
     sends, recvs, local,
 ):
-    moves = Moves(hidden, held, over, half_a, sends, recvs)
+    moves = Moves(hidden, held, over, half_a, back, sends, recvs)
     wait_barrier = moves.barrier()
     loads = {
         name: pltpu.make_async_copy(src, dst, local.at[i])
@@ -259,17 +265,19 @@
             loads["x"].wait()
             loads["wq"].wait()
             make_queries(held[:TOK, :], wq, queries)
-        elif verb == "kv":
+        elif verb == "turn":
+            loads["wv"].wait()
+            for i in range(D // 128):
+                wvt[i * 128 : (i + 1) * 128, :] = wv[:, i * 128 : (i + 1) * 128].T
+        elif verb in ("kv", "key", "value"):
             slots = args[0]
-            if slots == (OWN,):
-                loads["wk"].wait()
             rows = slice(slots[0] * TOK, (slots[-1] + 1) * TOK)
-            keys[rows, :] = project(held[rows, :], wk[...]).astype(BF)
-            if slots == (OWN,):
-                loads["wv"].wait()
-                for i in range(D // 128):
-                    wvt[i * 128 : (i + 1) * 128, :] = wv[:, i * 128 : (i + 1) * 128].T
-            values_t[:, rows] = lax.dot_general(wvt[...], held[rows, :], NT, preferred_element_type=F32).astype(BF)
+            if verb != "value":
+                if OWN in slots:
+                    loads["wk"].wait()
+                keys[rows, :] = project(held[rows, :], wk[...]).astype(BF)
+            if verb != "key":
+                values_t[:, rows] = lax.dot_general(wvt[...], held[rows, :], NT, preferred_element_type=F32).astype(BF)
         elif verb == "attend":
             slots = GROUPS[args[0]]
             attend(
@@ -285,16 +293,16 @@
 
 def per_device(hidden, pairs, w_query, w_key, w_value, w_out):
     any_space, vmem = pl.BlockSpec(memory_space=pl.ANY), pl.BlockSpec(memory_space=pltpu.VMEM)
-    half = sum(size for _, size, kind in CHUNKS if kind == "a")
+    half = sum(c[1] for c in CHUNKS if c[2] == "a")
     bf = lambda *shape: pltpu.VMEM(shape, BF)
     f32 = lambda *shape: pltpu.VMEM(shape, F32)
     return pl.pallas_call(
         kernel,
-        out_shape=jax.ShapeDtypeStruct((TOK, D), BF),
+        out_shape=pltpu.VMEM((TOK, D), BF),
         in_specs=[any_space, vmem, any_space, any_space, any_space, any_space],
         out_specs=vmem,
         scratch_shapes=[
-            bf(8 * TOK, D), bf(TOK, D), bf(TOK, half),
+            bf(8 * TOK, D), bf(TOK, D), bf(TOK, half), bf(TOK, D),
             bf(D, D), bf(D, D), bf(D, D), bf(D, D), bf(D, D),
             bf(HEADS * TOK, 256), bf(8 * TOK, D), bf(D, 8 * TOK),
             f32(HEADS, TOK), f32(HEADS, TOK), f32(HEADS, HEAD, TOK),

time: 40.6 us -> 35.8 us (0.88)
  Pallas kernels: 38.5 us -> 34.6 us
  local copies, waits for them, and re-layouts: 1.7 us -> 0.72 us
    pallas_call x1, Pallas kernels: 38.5 us -> 34.6 us  [per_device(): pl.pallas_call(kernel, out_shape=pltpu.VMEM((TOK, D), BF), in_specs=[any_...]
    unnamed x1, local copies, waits for them, and re-layouts: 1.7 us -> 0.72 us
where the time goes in v2:
time: 35.8 us; the launch traced here: 35.4 us
  Pallas kernels  34.6 us (97%)
  local copies, waits for them, and re-layouts  0.72 us (2%)
    pallas_call x1, Pallas kernels, per_device(): pl.pallas_call(kernel, out_shape=pltpu.VMEM((TOK, D), BF), in_specs=[any_...  34.6 us
    unnamed x1, local copies, waits for them, and re-layouts  0.72 us

profile of v2, /device:TPU:16, one launch (start us, length us, event | category | flops | bytes accessed | tf_op | source)
XLA Modules:
  0.0 35.4 jit_solution(9845776528406462365)
XLA Ops:
  0.0 34.6 %cross_view_attention.1 = bf16[128,1152]{1,0:T(8,128)(2,1)S(1)} custom-call(bf16[128,1152]{1,0:T(8,128)(2,1)} %hidden.1, s32[2,1024]{1,0:T(2,128)} %bitcast.1, bf16[1152,1152]{1,0:T(8,128)(2,1)} %w_query.1, bf16[1152,1152]{1,0:T(8,128)(2,1)} %w_key.1, bf16[1152,1152]{1,0:T(8,128)(2,1)} %w_value.1, bf16[1152,1152]{1,0:T(8,128)(2,1)} %w_out.1), custom_call_target="tpu_custom_call" | custom-call | tf_op jit(solution)/shard_map/cross_view_attention/pallas_call | solution.py:299
  34.7 0.7 %copy.8 = bf16[128,1152]{1,0:T(8,128)(2,1)} copy(bf16[128,1152]{1,0:T(8,128)(2,1)S(1)} %cross_view_attention.1) | data formatting | bytes 589824

commit v3 on v2

--- a/solution.py
+++ b/solution.py
@@ -17,10 +17,10 @@
 
 WINDOWS = ((0, (0, 1, 2)), (1, (3, 4)), (2, (5, 6)), (3, (7,)), (4, (8, 9)), (5, (10, 11)), (6, (12, 13)), (7, (14, 15)))
 
-OWN, SIB, REG1, FAR6, STEP1, NEAR6, REG2, HALF = range(8)
+OWN, SIB, NEAR6, FAR6, STEP1, REG1, REG2, HALF = range(8)
 
 CHUNKS = ((0, 640, "a", "z"), (640, 512, "b", "x"))
-GROUPS = ((OWN, SIB), (REG1, FAR6), (STEP1, NEAR6), (REG2,), (HALF,))
+GROUPS = ((OWN, SIB), (NEAR6, FAR6), (STEP1, REG1), (REG2, HALF))
 
 
 class Moves:
@@ -37,17 +37,15 @@
         other = 1 - col
         dy = 1 - 2 * xh
         self.cross = core != col
-        self.has_to = (y + dy >= 0) & (y + dy <= 3)
-        self.has_from = (y - dy >= 0) & (y - dy <= 3)
+        self.has_y = (y - dy >= 0) & (y - dy <= 3)
         sib, flip = at(0, col, 1 - core), at(0, other, core)
         xpair = (y * 2 + 1 - xh, z * 4 + other * 2 + core)
-        y_to = (jnp.clip(y + dy, 0, 3) * 2 + xh, p)
-        y_from = (jnp.clip(y - dy, 0, 3) * 2 + xh, p)
+        ypair = (jnp.clip(y - dy, 0, 3) * 2 + 1 - xh, z * 4 + other * 2 + core)
         step_to, step_from = at(-f, col, 1 - core), at(f, col, 1 - core)
 
         self.greet = [sib, flip, xpair, at(-f, col, core), at(f, col, core), at(2 * f, col, core), at(-2 * f, col, core), at(-2 * f, other, core)]
-        self.greet_if = [(jnp.logical_not(self.cross), step_from), (self.has_from, y_from)]
-        self.partners = 8 + self.cross.astype(jnp.int32) + self.has_to.astype(jnp.int32)
+        self.greet_if = [(jnp.logical_not(self.cross), step_from), (self.has_y, ypair)]
+        self.partners = 8 + self.cross.astype(jnp.int32) + self.has_y.astype(jnp.int32)
 
         place = lambda region, dev: region * 32 + dev[1]
         self.me = r * 32 + p
@@ -56,7 +54,7 @@
             SIB: place(r, sib),
             STEP1: jnp.where(self.cross, place(r, at(0, other, 1 - core)), place(r, at(f, other, 1 - core))),
             REG1: (y * 2 + 1 - xh) * 32 + p,
-            REG2: jnp.where(self.has_from, ((y - dy) * 2 + 1 - xh) * 32 + p, nowhere),
+            REG2: jnp.where(self.has_y, ((y - dy) * 2 + 1 - xh) * 32 + p, nowhere),
             NEAR6: place(r, at(-f, other, core)),
             FAR6: place(r, at(2 * f, other, core)),
             HALF: place(r, at(4, col, core)),
@@ -81,7 +79,7 @@
                 self.add(("near", k), cut(over), cut(slot(NEAR6)), at(f, col, core))
             self.add(("step", k), cut(over), cut(slot(STEP1)), sib, step_to)
             self.add(("xpair", k), cut(over), cut(slot(REG1)), xpair)
-            self.add(("ypair", k), cut(slot(REG1)), cut(slot(REG2)), y_to)
+            self.add(("ypair", k), cut(over), cut(slot(REG2)), ypair)
 
     def add(self, key, src, dst, device, device_if_cross=None):
         i = len(self.table)
@@ -101,7 +99,7 @@
             def _():
                 make(device).start()
         elif key[0] == "ypair":
-            @pl.when(self.has_to)
+            @pl.when(self.has_y)
             def _():
                 make(device).start()
         else:
@@ -110,7 +108,7 @@
     def arrived(self, key):
         make, device, _ = self.table[key]
         if key[0] == "ypair":
-            @pl.when(self.has_from)
+            @pl.when(self.has_y)
             def _():
                 make(device).wait_recv()
         else:
@@ -119,7 +117,7 @@
     def sent(self, key):
         make, device, _ = self.table[key]
         if key[0] == "ypair":
-            @pl.when(self.has_to)
+            @pl.when(self.has_y)
             def _():
                 make(device).wait_send()
         else:
@@ -204,19 +202,18 @@
     ("send", ("two", 0), ("flip", 1), ("flip", 0), ("back", 0), "sib"),
     "links", "q",
     ("key", (OWN,)), "turn",
-    ("relay", ("flip", 1), ("two", 1), ("near", 1), ("step", 1), ("xpair", 1)),
+    ("relay", ("flip", 1), ("two", 1), ("near", 1), ("step", 1), ("xpair", 1), ("ypair", 1)),
     ("relay", ("back", 0), ("near", 0)),
     ("value", (OWN,)),
     ("get", "sib"), ("kv", (SIB,)), ("attend", 0),
     ("relay", ("two", 0), ("four", 0), ("side", 0)),
-    ("relay", ("flip", 0), ("step", 0), ("xpair", 0)),
-    ("relay", ("xpair", 1), ("ypair", 1)),
+    ("relay", ("flip", 0), ("ypair", 0), ("step", 0), ("xpair", 0)),
+    ("get", ("near", 0), ("near", 1)), ("kv", (NEAR6,)),
     ("relay", ("two", 1), ("four", 1)),
-    ("relay", ("xpair", 0), ("ypair", 0)),
-    ("get", ("side", 0)), ("kv", (REG1, FAR6)), ("attend", 1),
-    ("get", ("step", 0), ("step", 1), ("near", 0), ("near", 1)), ("kv", (STEP1, NEAR6)), ("attend", 2),
-    ("get", ("ypair", 0), ("ypair", 1)), ("kv", (REG2,)), ("attend", 3),
-    ("get", ("four", 0), ("four", 1)), ("kv", (HALF,)), ("attend", 4),
+    ("get", ("side", 0)), ("kv", (FAR6,)), ("attend", 1),
+    ("get", ("step", 0), ("step", 1), ("xpair", 0), ("xpair", 1)), ("kv", (STEP1, REG1)), ("attend", 2),
+    ("get", ("ypair", 0), ("ypair", 1)), ("kv", (REG2,)),
+    ("get", ("four", 0), ("four", 1)), ("kv", (HALF,)), ("attend", 3),
     "finish",
 )
 
@@ -237,7 +234,7 @@
     for load in loads.values():
         load.start()
 
-    @pl.when(jnp.logical_not(moves.has_from))
+    @pl.when(jnp.logical_not(moves.has_y))
     def _():
         held[REG2 * TOK : (REG2 + 1) * TOK, :] = jnp.zeros((TOK, D), BF)
 

time: 35.8 us -> 35.4 us (0.989)
  no operation moved by 1% of the time
where the time goes in v3:
time: 35.4 us; the launch traced here: 35.3 us
  Pallas kernels  34.6 us (98%)
  local copies, waits for them, and re-layouts  0.72 us (2%)
    pallas_call x1, Pallas kernels, per_device(): pl.pallas_call(kernel, out_shape=pltpu.VMEM((TOK, D), BF), in_specs=[any_...  34.6 us
    unnamed x1, local copies, waits for them, and re-layouts  0.72 us

profile of v3, /device:TPU:16, one launch (start us, length us, event | category | flops | bytes accessed | tf_op | source)
XLA Modules:
  0.0 35.3 jit_solution(10669437326119322037)
XLA Ops:
  0.0 34.6 %cross_view_attention.1 = bf16[128,1152]{1,0:T(8,128)(2,1)S(1)} custom-call(bf16[128,1152]{1,0:T(8,128)(2,1)} %hidden.1, s32[2,1024]{1,0:T(2,128)} %bitcast.1, bf16[1152,1152]{1,0:T(8,128)(2,1)} %w_query.1, bf16[1152,1152]{1,0:T(8,128)(2,1)} %w_key.1, bf16[1152,1152]{1,0:T(8,128)(2,1)} %w_value.1, bf16[1152,1152]{1,0:T(8,128)(2,1)} %w_out.1), custom_call_target="tpu_custom_call" | custom-call | tf_op jit(solution)/shard_map/cross_view_attention/pallas_call | solution.py:296
  34.6 0.7 %copy.8 = bf16[128,1152]{1,0:T(8,128)(2,1)} copy(bf16[128,1152]{1,0:T(8,128)(2,1)S(1)} %cross_view_attention.1) | data formatting | bytes 589824

commit v4 on v3

--- a/solution.py
+++ b/solution.py
@@ -193,8 +193,8 @@
 
 def finish(totals, accum, mixed_t, wo):
     for h in range(HEADS):
-        mixed_t[h * HEAD : (h + 1) * HEAD, :] = accum[h] / totals[h : h + 1, :]
-    mixed = jnp.concatenate([mixed_t[t * 128 : (t + 1) * 128, :].T.astype(BF) for t in range(D // 128)], axis=1)
+        mixed_t[h * HEAD : (h + 1) * HEAD, :] = accum[h] * (1.0 / totals[h : h + 1, :])
+    mixed = jnp.concatenate([mixed_t[t * 128 : (t + 1) * 128, :].astype(BF).T for t in range(D // 128)], axis=1)
     return project(mixed, wo[...]).astype(BF)
 
 
@@ -213,7 +213,7 @@
     ("get", ("side", 0)), ("kv", (FAR6,)), ("attend", 1),
     ("get", ("step", 0), ("step", 1), ("xpair", 0), ("xpair", 1)), ("kv", (STEP1, REG1)), ("attend", 2),
     ("get", ("ypair", 0), ("ypair", 1)), ("kv", (REG2,)),
-    ("get", ("four", 0), ("four", 1)), ("kv", (HALF,)), ("attend", 3),
+    "wo", ("get", ("four", 0), ("four", 1)), ("kv", (HALF,)), ("attend", 3),
     "finish",
 )
 
@@ -281,8 +281,9 @@
                 args[0] == 0, slots[0] * TOK, [links[s] for s in slots],
                 queries, keys, values_t, tops, totals, accum, scores, weights,
             )
+        elif verb == "wo":
+            loads["wo"].wait()
         elif verb == "finish":
-            loads["wo"].wait()
             out[...] = finish(totals, accum, mixed_t, wo)
     for key in moves.table:
         moves.sent(key)

time: 35.4 us -> 35.2 us (level)
  no operation moved by 1% of the time
where the time goes in v4:
time: 35.2 us; the launch traced here: 35.1 us
  Pallas kernels  34.4 us (98%)
  local copies, waits for them, and re-layouts  0.72 us (2%)
    pallas_call x1, Pallas kernels, per_device(): pl.pallas_call(kernel, out_shape=pltpu.VMEM((TOK, D), BF), in_specs=[any_...  34.4 us
    unnamed x1, local copies, waits for them, and re-layouts  0.72 us

profile of v4, /device:TPU:16, one launch (start us, length us, event | category | flops | bytes accessed | tf_op | source)
XLA Modules:
  0.0 35.1 jit_solution(10603005416891901420)
XLA Ops:
  0.0 34.4 %cross_view_attention.1 = bf16[128,1152]{1,0:T(8,128)(2,1)S(1)} custom-call(bf16[128,1152]{1,0:T(8,128)(2,1)} %hidden.1, s32[2,1024]{1,0:T(2,128)} %bitcast.1, bf16[1152,1152]{1,0:T(8,128)(2,1)} %w_query.1, bf16[1152,1152]{1,0:T(8,128)(2,1)} %w_key.1, bf16[1152,1152]{1,0:T(8,128)(2,1)} %w_value.1, bf16[1152,1152]{1,0:T(8,128)(2,1)} %w_out.1), custom_call_target="tpu_custom_call" | custom-call | tf_op jit(solution)/shard_map/cross_view_attention/pallas_call | solution.py:297
  34.4 0.7 %copy.8 = bf16[128,1152]{1,0:T(8,128)(2,1)} copy(bf16[128,1152]{1,0:T(8,128)(2,1)S(1)} %cross_view_attention.1) | data formatting | bytes 589824
